TPU v7x, 256 devices: a whole 4x4x8 slice. The times are simulated.
256 devices in a mesh: rep: 8 (over y_lo, x), fsdp: 32 (over z, y_hi, core).
Axes of the slice: x: 4, y: 4 (y_hi: 2, y_lo: 2; y = y_hi * 2 + y_lo), z: 8, core: 2. Of those that a mesh axis runs over, the one named last changes fastest.
Arguments:
- hidden: bfloat16 [8, 12288, 8192], P('rep', 'fsdp'), may hold values from -6 to 6
- token_ids: int32 [8, 12288], P('rep', 'fsdp'), may hold values from 0 to 128255, as said below
- key_grad: bfloat16 [8, 12288, 512], P('rep', 'fsdp')
- weights: float32 [8, 8192, 512], P('rep', 'fsdp'), may hold values from -6 to 6
- first_moment: float32 [8, 8192, 512], P('rep', 'fsdp'), may hold values from -6 to 6
- second_moment: float32 [8, 8192, 512], P('rep', 'fsdp'), may hold values from 0.25 to 4
- anchor: float32 [8192, 512], P('fsdp'), may hold values from -6 to 6
- momentum: float32 [8192, 512], P('fsdp'), may hold values from -3 to 3
- fragment: int32 [1], replicated, may hold values from 0 to 1
- step_count: int32 [1], replicated, may hold values from 2 to 23
Outputs:
- keys: bfloat16 [8, 12288, 512], P('rep', 'fsdp')
- new_weights: float32 [8, 8192, 512], P('rep', 'fsdp')
- new_first: float32 [8, 8192, 512], P('rep', 'fsdp')
- new_second: float32 [8, 8192, 512], P('rep', 'fsdp')
- new_anchor: float32 [8192, 512], P('fsdp')
- new_momentum: float32 [8192, 512], P('fsdp')
Inputs may be any that keep to these rules, and one draw needn't show every extreme that they name: `token_ids`: 0 marks an empty slot; any other value is a vocabulary id below 128256.
All inputs are finite; a program needn't handle non-finite values.
Results may differ from a plain program's by a relative error of at most 0.0049.
Values may be sent and summed in bfloat16 or wider, within the bound.
A program may use at most 128 MiB of HBM per device.

v0:
```python
import math

import jax
import jax.numpy as jnp
from jax import lax
from jax.sharding import PartitionSpec as P

D = 8192
FRAGS = 2


BETA_ONE = 0.9
BETA_TWO = 0.95
EPSILON = 1e-08
INNER_LR = 0.1
WEIGHT_DECAY = 0.1
OUTER_LR = 0.7
OUTER_MOMENTUM = 0.9
MIX_LOCAL = 0.5


def on_device(
    hidden,
    token_ids,
    key_grad,
    weights,
    first_moment,
    second_moment,
    anchor,
    momentum,
    fragment,
    step_count,
):
    inverse_root = 1.0 / math.sqrt(D)
    tokens = hidden[0]
    own_weights = weights[0]
    key_width = own_weights.shape[1]
    frag_width = key_width // FRAGS
    first_col = fragment[0] * frag_width
    live_mask = token_ids[0] != 0
    local_count = jnp.sum(live_mask.astype(jnp.float32))
    group_count = lax.psum(local_count, "fsdp")
    wire_weights = own_weights.astype(jnp.bfloat16)
    feature_cols = tokens
    key_sums = jnp.dot(
        feature_cols,
        lax.all_gather(wire_weights, "fsdp", axis=0, tiled=True),
        preferred_element_type=jnp.float32,
    )
    new_keys = (key_sums * inverse_root).astype(jnp.bfloat16)
    masked = key_grad[0] * live_mask[:, None].astype(jnp.bfloat16)
    feature_cols = tokens
    grad_sum = lax.psum_scatter(
        lax.dot_general(
            feature_cols, masked, (((0,), (0,)), ((), ())), preferred_element_type=jnp.float32
        ),
        "fsdp",
        scatter_dimension=0,
        tiled=True,
    )
    gradient = grad_sum * inverse_root / group_count
    step_float = step_count[0].astype(jnp.float32)
    new_first = BETA_ONE * first_moment[0] + (1.0 - BETA_ONE) * gradient
    new_second = BETA_TWO * second_moment[0] + (1.0 - BETA_TWO) * gradient * gradient
    ratio_term = (
        new_first
        / (1.0 - BETA_ONE**step_float)
        / (jnp.sqrt(new_second / (1.0 - BETA_TWO**step_float)) + EPSILON)
    )
    stepped = own_weights - INNER_LR * (ratio_term + WEIGHT_DECAY * own_weights)
    own_delta = lax.dynamic_slice_in_dim(anchor - own_weights, first_col, frag_width, 1)
    delta = lax.psum(own_delta, "rep") / lax.axis_size("rep")
    momentum_cols = lax.dynamic_slice_in_dim(momentum, first_col, frag_width, 1)
    anchor_cols = lax.dynamic_slice_in_dim(anchor, first_col, frag_width, 1)
    moved_momentum = OUTER_MOMENTUM * momentum_cols + delta
    moved_anchor = anchor_cols - OUTER_LR * (delta + OUTER_MOMENTUM * moved_momentum)
    stepped_cols = lax.dynamic_slice_in_dim(stepped, first_col, frag_width, 1)
    mixed_cols = MIX_LOCAL * stepped_cols + (1.0 - MIX_LOCAL) * moved_anchor
    new_weights = lax.dynamic_update_slice_in_dim(stepped, mixed_cols, first_col, 1)
    new_anchor = lax.dynamic_update_slice_in_dim(anchor, moved_anchor, first_col, 1)
    new_momentum = lax.dynamic_update_slice_in_dim(momentum, moved_momentum, first_col, 1)
    return (
        new_keys[None],
        new_weights[None],
        new_first[None],
        new_second[None],
        new_anchor,
        new_momentum,
    )


def solution(mesh):
    return jax.shard_map(
        on_device,
        mesh=mesh,
        in_specs=(
            P("rep", "fsdp", None),
            P("rep", "fsdp"),
            P("rep", "fsdp", None),
            P("rep", "fsdp", None),
            P("rep", "fsdp", None),
            P("rep", "fsdp", None),
            P("fsdp", None),
            P("fsdp", None),
            P(),
            P(),
        ),
        out_specs=(
            P("rep", "fsdp", None),
            P("rep", "fsdp", None),
            P("rep", "fsdp", None),
            P("rep", "fsdp", None),
            P("fsdp", None),
            P("fsdp", None),
        ),
        check_vma=False,
    )
```

profile of v0, /device:TPU:1, one launch (start us, length us, event | category | flops | bytes accessed | tf_op | source)
XLA Modules:
  0.0 362.1 jit_solution(3876580256171411096)
XLA Ops:
  8.1 1.1 copy.38
  9.2 1.2 copy.39
  10.4 1.2 copy.16
  12.3 0.1 copy.28
  12.5 0.7 dynamic-slice_subtract_fusion
  13.3 0.7 bitcast_convert_fusion
  14.1 11.0 %convolution_bitcast_fusion = f32[8192,512]{0,1:T(8,128)} fusion(bf16[1,384,8192]{2,1,0:T(8,128)(2,1)} %param.10, bf16[1,384,512]{2,1,0:T(8,128)(2,1)S(1)} %copy-done.5, bf16[384]{0:T(512)(128)(2,1)S(1)} %fusion.16), kind=kOutput, calls=%fused_computation | convolution fusion | flops 3221422080 | bytes 23462656 | tf_op jit(solution)/shard_map/dot_general | solution.py:54
  25.1 0.6 fusion.17
  25.7 70.1 %psum.14 = f32[]{:T(128)} all-reduce(f32[]{:T(128)} %fusion.17), channel_id=1, replica_groups=mesh['rep'=8,'fsdp'=32] {'fsdp'}, use_global_device_ids=true, to_apply=%region_2.0 | all-reduce | flops 1 | bytes 8 | tf_op jit(solution)/shard_map/psum | solution.py:42
  95.9 0.2 copy.18
  96.8 0.2 copy.17
  97.1 0.1 copy.27
  97.2 1.0 multiply_add_fusion
  98.2 0.1 copy.23
  98.4 33.8 %all-gather.2.cloned.1.call-done = bf16[8192,512]{0,1:T(8,128)(2,1)} async-done(((bf16[256,512]{0,1:T(8,128)(2,1)}), bf16[8192,512]{0,1:T(8,128)(2,1)}) %all-gather.2.cloned.1.call-update) | async-done | bytes 8388624 | tf_op jit(solution)/shard_map/all_gather | solution.py:47
  132.3 9.4 %fusion.9 = bf16[1,384,512]{2,1,0:T(8,128)(2,1)} fusion(bf16[8192,512]{0,1:T(8,128)(2,1)} %all-gather.2.cloned.1.call-done, bf16[1,384,8192]{2,1,0:T(8,128)(2,1)} %param.10), kind=kOutput, calls=%fused_computation.6 | convolution fusion | flops 3221618688 | bytes 15073280 | tf_op jit(solution)/shard_map/dot_general | solution.py:45
  141.6 206.9 %reduce-scatter.2.cloned.1.call-done = f32[256,512]{0,1:T(8,128)} async-done(((f32[8192,512]{0,1:T(8,128)}), f32[256,512]{0,1:T(8,128)}) %reduce-scatter.2.cloned.1.call-update) | async-done | bytes 524304 | tf_op jit(solution)/shard_map/reduce_scatter | solution.py:53
  348.5 2.1 fusion.19
  350.7 0.1 bitcast_dynamic-update-slice_fusion
  350.8 1.0 copy.24
  351.8 1.0 copy.25
  352.8 1.0 copy.26
  353.8 0.1 copy.22
  353.9 0.7 constant_dynamic-update-slice_fusion
  (26 shorter events, 0.4 us)
Async XLA Ops:
  8.0 6.1 %copy-start.6 = (s32[1,384]{1,0:T(1,128)S(1)}, s32[1,384]{1,0:T(1,128)}, u32[]{:S(2)}) copy-start(s32[1,384]{1,0:T(1,128)} %param.11) | copy-start | bytes 4612
  8.0 6.1 %copy-start.5 = (bf16[1,384,512]{2,1,0:T(8,128)(2,1)S(1)}, bf16[1,384,512]{2,1,0:T(8,128)(2,1)}, u32[]{:S(2)}) copy-start(bf16[1,384,512]{2,1,0:T(8,128)(2,1)} %param.12) | copy-start | bytes 1179652
  8.0 89.2 %all-reduce.2.cloned.1.call-start = ((), (), s32[]{:S(2)}) async-start(), calls=%async_computation.3 | async-start | bytes 524288 | tf_op jit(solution)/shard_map/psum | solution.py:72
  9.2 16.0 %copy-start = (f32[256,512]{1,0:T(8,128)}, f32[256,512]{1,0:T(8,128)S(1)}, u32[]{:S(2)}) copy-start(f32[256,512]{1,0:T(8,128)S(1)} %copy.38) | copy-start | bytes 1572868
  13.2 119.0 %all-gather.2.cloned.1.call-start = ((), (), s32[]{:S(2)}) async-start(), calls=%async_computation.1 | async-start | bytes 8650752 | tf_op jit(solution)/shard_map/all_gather | solution.py:47
  14.0 334.5 %reduce-scatter.2.cloned.1.call-start = ((), (), s32[]{:S(2)}) async-start(), calls=%async_computation.2 | async-start | bytes 17301504 | tf_op jit(solution)/shard_map/reduce_scatter | solution.py:53
  25.1 70.8 %copy-start.3 = (f32[1,256,512]{2,1,0:T(8,128)S(1)}, f32[1,256,512]{2,1,0:T(8,128)}, u32[]{:S(2)}) copy-start(f32[1,256,512]{2,1,0:T(8,128)} %param.15) | copy-start | bytes 1572868
  25.1 71.7 %copy-start.4 = (f32[1,256,512]{2,1,0:T(8,128)S(1)}, f32[1,256,512]{2,1,0:T(8,128)}, u32[]{:S(2)}) copy-start(f32[1,256,512]{2,1,0:T(8,128)} %param.14) | copy-start | bytes 1572868
  98.4 43.3 %copy-start.1 = (f32[256,512]{1,0:T(8,128)}, f32[256,512]{1,0:T(8,128)S(1)}, u32[]{:S(2)}) copy-start(f32[256,512]{1,0:T(8,128)S(1)} %constant_dynamic-update-slice_fusion.1) | copy-start | bytes 1572868
  98.4 252.3 %copy-start.2 = (f32[256,256]{0,1:T(8,128)S(1)}, f32[256,256]{0,1:T(8,128)}, u32[]{:S(2)}) copy-start(f32[256,256]{0,1:T(8,128)} %all-reduce.2.cloned.1.call-done) | copy-start | bytes 786436
Sparse Core Ops, SparseCore 0:
  13.3 78.4 all-reduce.1
Sparse Core Ops, SparseCore 1:
  16.8 115.4 all-gather.1
  136.7 211.7 reduce-scatter.1
where the time goes:
time: 365 us; the launch traced here: 362 us
  waiting for transfers between devices  241 us (66%)
  blocking collectives  70.1 us (19%)
  matrix products  20.4 us (6%)
  between operations  17 us (5%)
  local copies, waits for them, and re-layouts  8.31 us (2%)
  other arithmetic  5.3 us (1%)
    reduce_scatter x1, waiting for transfers between devices, on_device(): lax.psum_scatter(lax.dot_general(feature_cols, masked, (((0,), (0,)), (()...  207 us
    psum x1, blocking collectives, on_device(): group_count = lax.psum(local_count, 'fsdp')  70.1 us
    all_gather x1, waiting for transfers between devices, on_device(): lax.all_gather(wire_weights, 'fsdp', axis=0, tiled=True)  33.8 us
    dot_general x1, matrix products, on_device(): lax.dot_general(feature_cols, masked, (((0,), (0,)), ((), ())), preferred...  11 us
    dot_general x1, matrix products, on_device(): jnp.dot(feature_cols, lax.all_gather(wire_weights, 'fsdp', axis=0, tiled=...  9.39 us
  transfers between devices with their start and end apart: 3, of which 2 were waited for; matrix products, arithmetic and copies ran while one was open for 6% of the time, Pallas kernels for 0%

commit v1 on v0

--- a/solution.py
+++ b/solution.py
@@ -3,11 +3,20 @@
 import jax
 import jax.numpy as jnp
 from jax import lax
+from jax.experimental import pallas as pl
+from jax.experimental.pallas import tpu as pltpu
 from jax.sharding import PartitionSpec as P
+
+MESH = pl.DeviceIdType.MESH
+BF16, F32 = jnp.bfloat16, jnp.float32
 
 D = 8192
 FRAGS = 2
-
+NZ = 8
+BLOCK = 256
+ROWS_A = 128
+ROWS_B = BLOCK - ROWS_A
+STEP = 32
 
 BETA_ONE = 0.9
 BETA_TWO = 0.95
@@ -17,6 +26,321 @@
 OUTER_LR = 0.7
 OUTER_MOMENTUM = 0.9
 MIX_LOCAL = 0.5
+
+
+def order(d):
+    return {4: 0, 3: 1, -3: 2, 2: 3, -2: 4, 1: 5, -1: 6, 0: 7}[d]
+
+
+def slot(d, p):
+    return 2 * order(d) + p
+
+
+def distance(o):
+    far = 4 - (o + 1) // 2
+    return jnp.where(o % 2 == 1, far, -far)
+
+
+def kernel(
+    hidden, masked, weights, grad_out, keys_out,
+    held, grads_in, parts, wire, acc, other, send_z, recv_z, send_y, recv_y, send_a, recv_a,
+    local_sem, send_sem, recv_sem, hid_send, hid_recv,
+):
+    tok = masked.shape[0]
+    width = masked.shape[1]
+    half = width // 2
+    rep = lax.axis_index("rep")
+    me = lax.axis_index("fsdp")
+    z, yh, core = me // 4, (me // 2) % 2, me % 2
+    mate = (rep, z * 4 + yh * 2 + (1 - core))
+    across = (rep, z * 4 + (1 - yh) * 2 + core)
+    up = (rep, lax.rem(z + 1, NZ) * 4 + yh * 2 + core)
+    down = (rep, lax.rem(z + NZ - 1, NZ) * 4 + yh * 2 + core)
+    toward = {1: up, -1: down}
+    rows_a, rows_b = pl.ds(0, ROWS_A), pl.ds(ROWS_A, ROWS_B)
+    cols = {1: pl.ds(0, half), -1: pl.ds(half, half)}
+    copies = {}
+
+    def block_cols(q, c):
+        d, p = distance(q // 2), q % 2
+        zz = lax.rem(z + d + 2 * NZ, NZ)
+        yy = lax.rem(yh + p, 2)
+        return pl.ds(pl.multiple_of((zz * 4 + yy * 2 + c) * BLOCK, BLOCK), BLOCK)
+
+    def hidden_local(q):
+        return pltpu.make_async_copy(
+            hidden.at[:, block_cols(q, core)], held.at[q, pl.ds(0, tok)], local_sem.at[q]
+        )
+
+    def hidden_remote(q):
+        return pltpu.make_async_remote_copy(
+            src_ref=hidden.at[:, block_cols(q, 1 - core)],
+            dst_ref=held.at[q, pl.ds(tok, tok)],
+            send_sem=hid_send.at[q],
+            recv_sem=hid_recv.at[q],
+            device_id=mate,
+            device_id_type=MESH,
+        )
+
+    def send(name, src, dst, target):
+        index = len(copies)
+        copies[name] = pltpu.make_async_remote_copy(
+            src_ref=src,
+            dst_ref=dst,
+            send_sem=send_sem.at[index],
+            recv_sem=recv_sem.at[index],
+            device_id=target,
+            device_id_type=MESH,
+        )
+        copies[name].start()
+
+    def arrived(name):
+        copies[name].wait_recv()
+
+    def loop_rows(count, body):
+        @pl.loop(0, count // STEP)
+        def _(i):
+            body(pl.multiple_of(i * STEP, STEP))
+
+    @pl.loop(0, 16)
+    def _(q):
+        hidden_local(q).start()
+
+    barrier = pltpu.get_barrier_semaphore()
+    for target in (mate, across, up, down):
+        pl.semaphore_signal(barrier, inc=1, device_id=target, device_id_type=MESH)
+    own = slot(0, 0)
+
+    def cast(r):
+        wire[own, pl.ds(r, STEP)] = weights[pl.ds(r, STEP)].astype(BF16)
+
+    loop_rows(BLOCK, cast)
+
+    def take(r):
+        grads_in[pl.ds(r, STEP)] = masked[pl.ds(r, STEP)]
+
+    loop_rows(tok, take)
+    pl.semaphore_wait(barrier, 4)
+
+    send("ay0", wire.at[own, rows_a], wire.at[slot(0, 1), rows_a], across)
+    for s in (1, -1):
+        send(("az", s, 1, 0), wire.at[own], wire.at[slot(-s, 0)], toward[s])
+    send("ayB0", wire.at[own, rows_b], wire.at[slot(0, 1), rows_b], across)
+    send("mask", grads_in.at[pl.ds(0, tok)], grads_in.at[pl.ds(tok, tok)], mate)
+
+    @pl.loop(0, 16)
+    def _(q):
+        hidden_remote(q).start()
+
+    def gather_hop(k, p):
+        for s in (1, -1):
+            src = slot(-s * (k - 1), p)
+            dst = slot(4 if k == 4 else -s * k, p)
+            rows = pl.ds(0, BLOCK) if p == 0 else rows_a
+            if k > 1:
+                arrived(("az", s, k - 1, p))
+            if k == 4:
+                send(("az", s, k, p), wire.at[src, rows, cols[s]], wire.at[dst, rows, cols[s]], toward[s])
+            else:
+                send(("az", s, k, p), wire.at[src, rows], wire.at[dst, rows], toward[s])
+            if p == 0 and k > 1:
+                send(("ayB", src), wire.at[src, rows_b], wire.at[src + 1, rows_b], across)
+
+    def gather_step(k):
+        gather_hop(k, 0)
+        gather_hop(k, 1)
+
+    def gradient(*distances):
+        first = order(distances[0])
+
+        @pl.loop(2 * first, 2 * (first + len(distances)))
+        def _(q):
+            hidden_local(q).wait()
+            hidden_remote(q).wait_recv()
+            parts[q] = lax.dot_general(
+                held[q], grads_in[...], (((0,), (0,)), ((), ())), preferred_element_type=F32
+            )
+
+        for d in distances:
+            o = order(d)
+
+            def stage(r, o=o):
+                send_y[o, pl.ds(r, STEP)] = parts[2 * o + 1, pl.ds(ROWS_A + r, STEP)].astype(BF16)
+
+            loop_rows(ROWS_B, stage)
+            send(("ry", d), send_y.at[o], recv_y.at[o], across)
+
+    def reduce_far(p):
+        for s in (1, -1):
+            def stage(r, s=s):
+                here = parts[slot(4, p), pl.ds(r, STEP), cols[s]]
+                send_z[0 if s == 1 else 1, 3, pl.ds(p * BLOCK + r, STEP), cols[s]] = here.astype(BF16)
+
+            def stage_b(r, s=s):
+                here = parts[slot(4, p), pl.ds(ROWS_A + r, STEP), cols[s]]
+                here = here + recv_y[order(4), pl.ds(r, STEP), cols[s]].astype(F32)
+                send_z[0 if s == 1 else 1, 3, pl.ds(ROWS_A + r, STEP), cols[s]] = here.astype(BF16)
+
+            loop_rows(ROWS_A, stage)
+            if p == 0:
+                if s == 1:
+                    arrived(("ry", 4))
+                loop_rows(ROWS_B, stage_b)
+            rows = pl.ds(0, BLOCK) if p == 0 else pl.ds(BLOCK, ROWS_A)
+            w = 0 if s == 1 else 1
+            send(("rz", s, 4, p), send_z.at[w, 3, rows, cols[s]], recv_z.at[w, 3, rows, cols[s]], toward[s])
+
+    def reduce_hop(d, p):
+        for s in (1, -1):
+            w = 0 if s == 1 else 1
+            arrived(("rz", s, d + 1, p))
+            if p == 0:
+                arrived(("ry", s * d))
+
+            def put(r, base, with_y, s=s, w=w):
+                here = parts[slot(s * d, p), pl.ds(base + r, STEP)]
+                at = pl.ds(p * BLOCK + base + r, STEP)
+                if with_y:
+                    here = here + recv_y[order(s * d), pl.ds(r, STEP)].astype(F32)
+                if d == 3:
+                    lo = 0 if s == 1 else half
+                    there = recv_z[w, d, at, cols[s]].astype(F32)
+                    summed = here[:, lo:lo + half] + there
+                    send_z[w, d - 1, at, cols[s]] = summed.astype(BF16)
+                    send_z[w, d - 1, at, cols[-s]] = here[:, half - lo:2 * half - lo].astype(BF16)
+                else:
+                    there = recv_z[w, d, at].astype(F32)
+                    send_z[w, d - 1, at] = (here + there).astype(BF16)
+
+            loop_rows(ROWS_A, lambda r: put(r, 0, False))
+            if p == 0:
+                loop_rows(ROWS_B, lambda r: put(r, ROWS_A, True))
+            rows = pl.ds(0, BLOCK) if p == 0 else pl.ds(BLOCK, ROWS_A)
+            send(("rz", s, d, p), send_z.at[w, d - 1, rows], recv_z.at[w, d - 1, rows], toward[s])
+
+    def keys(*distances):
+        for d in distances:
+            q = slot(d, 0)
+            if d == 0:
+                arrived("ayB0")
+            elif d == 4:
+                arrived(("ayB", 4, 1))
+                arrived(("ayB", 4, -1))
+            else:
+                arrived(("ayB", q))
+            acc[...] += jnp.dot(held[q], wire[q], preferred_element_type=F32) + jnp.dot(
+                held[q + 1], wire[q + 1], preferred_element_type=F32
+            )
+
+    arrived("mask")
+    gradient(4)
+    reduce_far(1)
+    arrived("ay0")
+    gather_hop(1, 1)
+    gradient(3, -3)
+    reduce_far(0)
+    gather_step(2)
+    gradient(2, -2)
+    reduce_hop(3, 1)
+    reduce_hop(3, 0)
+    gather_step(3)
+    gradient(1, -1, 0)
+    acc[...] = jnp.zeros_like(acc)
+    reduce_hop(2, 1)
+    reduce_hop(2, 0)
+    gather_step(4)
+    keys(0)
+    reduce_hop(1, 1)
+    reduce_hop(1, 0)
+    for s in (1, -1):
+        arrived(("az", s, 4, 0))
+        src = slot(4, 0)
+        send(("ayB", 4, s), wire.at[src, rows_b, cols[s]], wire.at[src + 1, rows_b, cols[s]], across)
+    keys(1, -1, 2, -2, 3, -3)
+
+    for s in (1, -1):
+        arrived(("rz", s, 1, 1))
+
+    def close_a(r):
+        at = pl.ds(BLOCK + r, STEP)
+        total = parts[slot(0, 1), pl.ds(r, STEP)] + recv_z[0, 0, at].astype(F32) + recv_z[1, 0, at].astype(F32)
+        send_a[pl.ds(r, STEP)] = total.astype(BF16)
+
+    loop_rows(ROWS_A, close_a)
+    send("rya", send_a, recv_a, across)
+    for s in (1, -1):
+        arrived(("az", s, 4, 1))
+    keys(4)
+    send("keys", acc.at[pl.ds(tok, tok)], other, mate)
+    for s in (1, -1):
+        arrived(("rz", s, 1, 0))
+    arrived(("ry", 0))
+
+    def close_b(r):
+        at = pl.ds(ROWS_A + r, STEP)
+        total = parts[slot(0, 0), at] + recv_y[order(0), pl.ds(r, STEP)].astype(F32)
+        grad_out[at] = total + recv_z[0, 0, at].astype(F32) + recv_z[1, 0, at].astype(F32)
+
+    loop_rows(ROWS_B, close_b)
+    arrived("rya")
+
+    def close_all(r):
+        at = pl.ds(r, STEP)
+        total = parts[slot(0, 0), at] + recv_a[at].astype(F32)
+        grad_out[at] = total + recv_z[0, 0, at].astype(F32) + recv_z[1, 0, at].astype(F32)
+
+    loop_rows(ROWS_A, close_all)
+    arrived("keys")
+
+    def close_keys(r):
+        at = pl.ds(r, STEP)
+        keys_out[at] = ((acc[at] + other[at]) * (1.0 / math.sqrt(D))).astype(BF16)
+
+    loop_rows(tok, close_keys)
+    for copy in copies.values():
+        copy.wait_send()
+
+    @pl.loop(0, 16)
+    def _(q):
+        hidden_remote(q).wait_send()
+
+
+def exchange(hidden, masked, weights):
+    tok, width = masked.shape
+    vmem = pl.BlockSpec(memory_space=pltpu.VMEM)
+    count = 80
+    return pl.pallas_call(
+        kernel,
+        out_shape=(
+            jax.ShapeDtypeStruct((BLOCK, width), F32),
+            jax.ShapeDtypeStruct((tok, width), BF16),
+        ),
+        in_specs=[pl.BlockSpec(memory_space=pl.ANY), vmem, vmem],
+        out_specs=(vmem, vmem),
+        scratch_shapes=[
+            pltpu.VMEM((16, 2 * tok, BLOCK), BF16),
+            pltpu.VMEM((2 * tok, width), BF16),
+            pltpu.VMEM((16, BLOCK, width), F32),
+            pltpu.VMEM((16, BLOCK, width), BF16),
+            pltpu.VMEM((2 * tok, width), F32),
+            pltpu.VMEM((tok, width), F32),
+            pltpu.VMEM((2, 4, BLOCK + ROWS_A, width), BF16),
+            pltpu.VMEM((2, 4, BLOCK + ROWS_A, width), BF16),
+            pltpu.VMEM((8, ROWS_B, width), BF16),
+            pltpu.VMEM((8, ROWS_B, width), BF16),
+            pltpu.VMEM((ROWS_A, width), BF16),
+            pltpu.VMEM((ROWS_A, width), BF16),
+            pltpu.SemaphoreType.DMA((16,)),
+            pltpu.SemaphoreType.DMA((count,)),
+            pltpu.SemaphoreType.DMA((count,)),
+            pltpu.SemaphoreType.DMA((16,)),
+            pltpu.SemaphoreType.DMA((16,)),
+        ],
+        compiler_params=pltpu.CompilerParams(
+            collective_id=0, has_side_effects=True, vmem_limit_bytes=56 * 2**20
+        ),
+        cost_estimate=pl.CostEstimate(flops=13 * 10**9, bytes_accessed=16 * 2**20, transcendentals=0),
+    )(hidden, masked, weights)
 
 
 def on_device(
@@ -32,34 +356,19 @@
     step_count,
 ):
     inverse_root = 1.0 / math.sqrt(D)
-    tokens = hidden[0]
     own_weights = weights[0]
     key_width = own_weights.shape[1]
     frag_width = key_width // FRAGS
     first_col = fragment[0] * frag_width
     live_mask = token_ids[0] != 0
-    local_count = jnp.sum(live_mask.astype(jnp.float32))
+    local_count = jnp.sum(live_mask.astype(F32))
     group_count = lax.psum(local_count, "fsdp")
-    wire_weights = own_weights.astype(jnp.bfloat16)
-    feature_cols = tokens
-    key_sums = jnp.dot(
-        feature_cols,
-        lax.all_gather(wire_weights, "fsdp", axis=0, tiled=True),
-        preferred_element_type=jnp.float32,
-    )
-    new_keys = (key_sums * inverse_root).astype(jnp.bfloat16)
-    masked = key_grad[0] * live_mask[:, None].astype(jnp.bfloat16)
-    feature_cols = tokens
-    grad_sum = lax.psum_scatter(
-        lax.dot_general(
-            feature_cols, masked, (((0,), (0,)), ((), ())), preferred_element_type=jnp.float32
-        ),
-        "fsdp",
-        scatter_dimension=0,
-        tiled=True,
-    )
+    own_delta = lax.dynamic_slice_in_dim(anchor - own_weights, first_col, frag_width, 1)
+    delta = lax.psum(own_delta, "rep") / lax.axis_size("rep")
+    masked = key_grad[0] * live_mask[:, None].astype(BF16)
+    grad_sum, new_keys = exchange(hidden[0], masked, own_weights)
     gradient = grad_sum * inverse_root / group_count
-    step_float = step_count[0].astype(jnp.float32)
+    step_float = step_count[0].astype(F32)
     new_first = BETA_ONE * first_moment[0] + (1.0 - BETA_ONE) * gradient
     new_second = BETA_TWO * second_moment[0] + (1.0 - BETA_TWO) * gradient * gradient
     ratio_term = (
@@ -68,8 +377,6 @@
         / (jnp.sqrt(new_second / (1.0 - BETA_TWO**step_float)) + EPSILON)
     )
     stepped = own_weights - INNER_LR * (ratio_term + WEIGHT_DECAY * own_weights)
-    own_delta = lax.dynamic_slice_in_dim(anchor - own_weights, first_col, frag_width, 1)
-    delta = lax.psum(own_delta, "rep") / lax.axis_size("rep")
     momentum_cols = lax.dynamic_slice_in_dim(momentum, first_col, frag_width, 1)
     anchor_cols = lax.dynamic_slice_in_dim(anchor, first_col, frag_width, 1)
     moved_momentum = OUTER_MOMENTUM * momentum_cols + delta

time: 365 us -> 171 us (0.47)
  waiting for transfers between devices: 241 us -> 0.04 us
  Pallas kernels: 0 us -> 70.3 us
  matrix products: 20.4 us -> 0 us
  other arithmetic: 5.3 us -> 11 us
  local copies, waits for them, and re-layouts: 8.31 us -> 3.21 us
    reduce_scatter x1 -> x0, waiting for transfers between devices: 207 us -> none  [on_device(): lax.psum_scatter(lax.dot_general(feature_cols, masked, (((0,), (0,)), (()...]
    pallas_call x0 -> x1, Pallas kernels: none -> 70.3 us  [exchange(): pl.pallas_call(kernel, out_shape=(jax.ShapeDtypeStruct((BLOCK, width), F3...]
    all_gather x1 -> x0, waiting for transfers between devices: 33.8 us -> none  [on_device(): lax.all_gather(wire_weights, 'fsdp', axis=0, tiled=True)]
    dot_general x2 -> x0, matrix products: 20.4 us -> none  [the longest x1 11 us: on_device(): lax.dot_general(feature_cols, masked, (((0,), (0,)), ((), ())), preferred...]
    unnamed x25 -> x18, local copies, waits for them, and re-layouts: 7.25 us -> 3.21 us
  transfers between devices with their start and end apart: 3 -> 1, of which waited for: 2 -> 0; matrix products, arithmetic and copies ran while one was open for 6% -> 4% of each run, Pallas kernels for 0% -> 41%
where the time goes in v1:
time: 171 us; the launch traced here: 170 us
  Pallas kernels  70.3 us (41%)
  blocking collectives  69.8 us (41%)
  between operations  15.5 us (9%)
  other arithmetic  11 us (6%)
  local copies, waits for them, and re-layouts  3.21 us (2%)
    pallas_call x1, Pallas kernels, exchange(): pl.pallas_call(kernel, out_shape=(jax.ShapeDtypeStruct((BLOCK, width), F3...  70.3 us
    psum x1, blocking collectives, on_device(): group_count = lax.psum(local_count, 'fsdp')  69.8 us
  transfers between devices with their start and end apart: 1, of which 0 were waited for; matrix products, arithmetic and copies ran while one was open for 4% of the time, Pallas kernels for 41%

profile of v1, /device:TPU:1, one launch (start us, length us, event | category | flops | bytes accessed | tf_op | source)
XLA Modules:
  0.0 170.0 jit_solution(371401169526698522)
XLA Ops:
  7.2 0.0 all-reduce.2.cloned.1.call-start
  7.2 1.0 copy.25
  8.3 1.0 copy.26
  10.0 1.7 dynamic-slice_subtract_fusion
  11.6 0.0 all-reduce.2.cloned.1.call-update
  11.7 1.3 fusion.3
  13.0 0.7 fusion.2
  14.4 69.8 %psum.14 = f32[]{:T(128)} all-reduce(f32[]{:T(128)} %fusion.3), channel_id=1, replica_groups=mesh['rep'=8,'fsdp'=32] {'fsdp'}, use_global_device_ids=true, to_apply=%region_1.0 | all-reduce | flops 1 | bytes 8 | tf_op jit(solution)/shard_map/psum | solution.py:365
  84.2 1.9 %bitcast_multiply_fusion.masked = bf16[384,512]{1,0:T(8,128)(2,1)} fusion(bf16[1,384,512]{2,1,0:T(8,128)(2,1)} %param.12, bf16[384]{0:T(512)(128)(2,1)S(1)} %fusion.2), kind=kLoop, calls=%fused_computation.5 | loop fusion | flops 196608 | bytes 787200 | tf_op jit(solution)/shard_map/mul | solution.py:368
  86.1 70.3 %shard_map.145 = (f32[256,512]{1,0:T(8,128)}, bf16[384,512]{1,0:T(8,128)(2,1)}) custom-call(bf16[384,8192]{1,0:T(8,128)(2,1)} %bitcast.32, bf16[384,512]{1,0:T(8,128)(2,1)} %bitcast_multiply_fusion.masked, f32[256,512]{1,0:T(8,128)} %bitcast.30), custom_call_target="tpu_custom_call" | custom-call | flops 12999999488 | bytes 16777216 | tf_op jit(solution)/shard_map/pallas_call | solution.py:312
  156.5 0.0 copy-start.6
  156.5 0.0 copy-done.2
  156.5 0.0 copy-done.4
  156.5 0.0 copy-done.5
  156.5 3.1 %fusion.5 = (f32[1,256,512]{2,1,0:T(8,128)}, f32[256,512]{1,0:T(8,128)S(1)}, f32[1,256,512]{2,1,0:T(8,128)}) fusion(f32[]{:T(128)} %psum.14, f32[256,512]{1,0:T(8,128)} %get-tuple-element.9, f32[1,256,512]{2,1,0:T(8,128)S(1)} %copy-done.4, f32[]{:T(128)} %bitcast.7, f32[]{:T(128)} %bitcast.5, f32[1,256,512]{2,1,0:T(8,128)S(1)} %copy-done.5, ...), kind=kLoop, calls=%fused_computation.17 | loop fusion | flops 2228224 | bytes 3670028 | tf_op jit(solution)/shard_map/broadcast_in_dim | solution.py:393
  159.7 0.0 all-reduce.2.cloned.1.call-done
  159.7 1.1 bitcast_dynamic-update-slice_fusion
  160.8 0.0 copy-start.3
  160.8 1.3 fusion.1
  162.0 0.0 copy-start
  162.1 0.0 copy-start.1
  162.1 0.8 copy.27
  162.9 0.1 copy-done
  163.0 0.2 copy-done.1
  (6 shorter events, 0.0 us)
Async XLA Ops:
  7.2 152.5 %all-reduce.2.cloned.1.call-start = ((), (), s32[]{:S(2)}) async-start(), calls=%async_computation | async-start | bytes 524288 | tf_op jit(solution)/shard_map/psum | solution.py:367
  86.1 70.4 %copy-start.2 = (f32[1,256,512]{2,1,0:T(8,128)S(1)}, f32[1,256,512]{2,1,0:T(8,128)}, u32[]{:S(2)}) copy-start(f32[1,256,512]{2,1,0:T(8,128)} %param.13) | copy-start | bytes 1572868
  86.1 70.4 %copy-start.4 = (f32[1,256,512]{2,1,0:T(8,128)S(1)}, f32[1,256,512]{2,1,0:T(8,128)}, u32[]{:S(2)}) copy-start(f32[1,256,512]{2,1,0:T(8,128)} %param.15) | copy-start | bytes 1572868
  86.1 70.4 %copy-start.5 = (f32[1,256,512]{2,1,0:T(8,128)S(1)}, f32[1,256,512]{2,1,0:T(8,128)}, u32[]{:S(2)}) copy-start(f32[1,256,512]{2,1,0:T(8,128)} %param.14) | copy-start | bytes 1572868
  156.5 5.6 %copy-start.6 = (bf16[384,512]{1,0:T(8,128)(2,1)S(1)}, bf16[384,512]{1,0:T(8,128)(2,1)}, u32[]{:S(2)}) copy-start(bf16[384,512]{1,0:T(8,128)(2,1)} %get-tuple-element.8) | copy-start | bytes 1179652
  160.8 2.1 %copy-start.3 = (f32[1,256,512]{2,1,0:T(8,128)}, f32[1,256,512]{2,1,0:T(8,128)S(1)}, u32[]{:S(2)}) copy-start(f32[1,256,512]{2,1,0:T(8,128)S(1)} %bitcast_dynamic-update-slice_fusion) | copy-start | bytes 1572868
  162.0 0.9 copy-start
  162.1 1.1 copy-start.1
Sparse Core Ops, SparseCore 0:
  11.8 77.9 all-reduce.1

commit v2 on v1

--- a/solution.py
+++ b/solution.py
@@ -13,10 +13,11 @@
 D = 8192
 FRAGS = 2
 NZ = 8
+NX = 4
 BLOCK = 256
-ROWS_A = 128
+ROWS_A = 112
 ROWS_B = BLOCK - ROWS_A
-STEP = 32
+STEP = 16
 
 BETA_ONE = 0.9
 BETA_TWO = 0.95
@@ -42,21 +43,25 @@
 
 
 def kernel(
-    hidden, masked, weights, grad_out, keys_out,
+    hidden, tokens, key_grad, weights, anchor, fragment, grad_out, keys_out, delta_out,
     held, grads_in, parts, wire, acc, other, send_z, recv_z, send_y, recv_y, send_a, recv_a,
-    local_sem, send_sem, recv_sem, hid_send, hid_recv,
+    raw_grad, raw_weights, raw_anchor, raw_tokens, differ, from_x, piece, from_y, delta, counts, count_mate, count_pair, count_across,
+    local_sem, raw_sem, send_sem, recv_sem, hid_send, hid_recv,
 ):
-    tok = masked.shape[0]
-    width = masked.shape[1]
+    tok, width = key_grad.shape
     half = width // 2
+    quarter = BLOCK // NX
     rep = lax.axis_index("rep")
     me = lax.axis_index("fsdp")
     z, yh, core = me // 4, (me // 2) % 2, me % 2
+    yl, x = rep // NX, rep % NX
     mate = (rep, z * 4 + yh * 2 + (1 - core))
     across = (rep, z * 4 + (1 - yh) * 2 + core)
     up = (rep, lax.rem(z + 1, NZ) * 4 + yh * 2 + core)
     down = (rep, lax.rem(z + NZ - 1, NZ) * 4 + yh * 2 + core)
     toward = {1: up, -1: down}
+    beside = ((1 - yl) * NX + x, me)
+    along = {e: (yl * NX + lax.rem(x + e, NX), me) for e in range(1, NX)}
     rows_a, rows_b = pl.ds(0, ROWS_A), pl.ds(ROWS_A, ROWS_B)
     cols = {1: pl.ds(0, half), -1: pl.ds(half, half)}
     copies = {}
@@ -102,35 +107,91 @@
         def _(i):
             body(pl.multiple_of(i * STEP, STEP))
 
+    loads = [
+        pltpu.make_async_copy(src, dst, raw_sem.at[i])
+        for i, (src, dst) in enumerate(((weights, raw_weights), (anchor, raw_anchor), (key_grad, raw_grad), (tokens, raw_tokens)))
+    ]
+    for load in loads:
+        load.start()
+
     @pl.loop(0, 16)
     def _(q):
         hidden_local(q).start()
 
     barrier = pltpu.get_barrier_semaphore()
-    for target in (mate, across, up, down):
+    partners = (mate, across, up, down, beside, *along.values())
+    for target in partners:
         pl.semaphore_signal(barrier, inc=1, device_id=target, device_id_type=MESH)
     own = slot(0, 0)
+    loads[0].wait()
 
     def cast(r):
-        wire[own, pl.ds(r, STEP)] = weights[pl.ds(r, STEP)].astype(BF16)
+        wire[own, pl.ds(r, STEP)] = raw_weights[pl.ds(r, STEP)].astype(BF16)
 
     loop_rows(BLOCK, cast)
-
-    def take(r):
-        grads_in[pl.ds(r, STEP)] = masked[pl.ds(r, STEP)]
-
-    loop_rows(tok, take)
-    pl.semaphore_wait(barrier, 4)
+    loads[1].wait()
+    in_second = fragment[0].astype(F32)
+
+    def subtract(r):
+        at = pl.ds(r, STEP)
+        gap = raw_anchor[at] - raw_weights[at]
+        differ[at] = gap[:, :half] * (1.0 - in_second) + gap[:, half:] * in_second
+
+    loop_rows(BLOCK, subtract)
+    loads[2].wait()
+    loads[3].wait()
+    live = (raw_tokens[...] != 0).astype(F32)
+    live_rows = jnp.transpose(jnp.broadcast_to(live, (128, tok))).astype(BF16)
+    for j in range(width // 128):
+        at = pl.ds(j * 128, 128)
+        grads_in[pl.ds(0, tok), at] = raw_grad[:, at] * live_rows
+    count_pair[...] = jnp.broadcast_to(jnp.sum(live, axis=1, keepdims=True), count_pair.shape)
+    pl.semaphore_wait(barrier, len(partners))
 
     send("ay0", wire.at[own, rows_a], wire.at[slot(0, 1), rows_a], across)
     for s in (1, -1):
         send(("az", s, 1, 0), wire.at[own], wire.at[slot(-s, 0)], toward[s])
     send("ayB0", wire.at[own, rows_b], wire.at[slot(0, 1), rows_b], across)
+    send("count_mate", count_pair, count_mate, mate)
     send("mask", grads_in.at[pl.ds(0, tok)], grads_in.at[pl.ds(tok, tok)], mate)
 
     @pl.loop(0, 16)
     def _(q):
         hidden_remote(q).start()
+
+    for e in range(1, NX):
+        at = pl.ds(pl.multiple_of(lax.rem(x + e, NX) * quarter, quarter), quarter)
+        send(("dx", e), differ.at[at], from_x.at[e - 1], along[e])
+    own_quarter = pl.ds(pl.multiple_of(x * quarter, quarter), quarter)
+
+    def difference_x():
+        for e in range(1, NX):
+            arrived(("dx", e))
+        piece[...] = differ[own_quarter] + from_x[0] + from_x[1] + from_x[2]
+        send("dy", piece, from_y, beside)
+
+    def difference_y():
+        arrived("dy")
+        delta[own_quarter] = (piece[...] + from_y[...]) * (1.0 / 8.0)
+        for e in range(1, NX):
+            send(("dg", e), delta.at[own_quarter], delta.at[own_quarter], along[e])
+
+    def count_chip():
+        arrived("count_mate")
+        counts[0] = count_pair[...] + count_mate[...]
+        send("count_across", counts.at[0], count_across, across)
+
+    def count_column():
+        arrived("count_across")
+        counts[1] = counts[0] + count_across[...]
+        for s in (1, -1):
+            send(("cz", s, 1), counts.at[1], counts.at[1 + (-s) % NZ], toward[s])
+
+    def count_hop(k):
+        for s in (1, -1):
+            arrived(("cz", s, k - 1))
+            if k < 4 or s == 1:
+                send(("cz", s, k), counts.at[1 + (-s * (k - 1)) % NZ], counts.at[1 + (-s * k) % NZ], toward[s])
 
     def gather_hop(k, p):
         for s in (1, -1):
@@ -237,26 +298,41 @@
     reduce_far(1)
     arrived("ay0")
     gather_hop(1, 1)
+    count_chip()
     gradient(3, -3)
     reduce_far(0)
     gather_step(2)
+    difference_x()
+    count_column()
     gradient(2, -2)
     reduce_hop(3, 1)
     reduce_hop(3, 0)
     gather_step(3)
+    count_hop(2)
+    difference_y()
     gradient(1, -1, 0)
     acc[...] = jnp.zeros_like(acc)
     reduce_hop(2, 1)
     reduce_hop(2, 0)
     gather_step(4)
+    count_hop(3)
     keys(0)
     reduce_hop(1, 1)
     reduce_hop(1, 0)
+    count_hop(4)
     for s in (1, -1):
         arrived(("az", s, 4, 0))
         src = slot(4, 0)
         send(("ayB", 4, s), wire.at[src, rows_b, cols[s]], wire.at[src + 1, rows_b, cols[s]], across)
     keys(1, -1, 2, -2, 3, -3)
+    arrived(("cz", 1, 4))
+    group_count = counts[1]
+    for i in range(1, NZ):
+        group_count = group_count + counts[1 + i]
+    scale = ((1.0 / math.sqrt(D)) / group_count)[0:1, 0:1]
+    for e in range(1, NX):
+        arrived(("dg", e))
+    delta_out[...] = delta[...]
 
     for s in (1, -1):
         arrived(("rz", s, 1, 1))
@@ -279,7 +355,7 @@
     def close_b(r):
         at = pl.ds(ROWS_A + r, STEP)
         total = parts[slot(0, 0), at] + recv_y[order(0), pl.ds(r, STEP)].astype(F32)
-        grad_out[at] = total + recv_z[0, 0, at].astype(F32) + recv_z[1, 0, at].astype(F32)
+        grad_out[at] = (total + recv_z[0, 0, at].astype(F32) + recv_z[1, 0, at].astype(F32)) * scale
 
     loop_rows(ROWS_B, close_b)
     arrived("rya")
@@ -287,7 +363,7 @@
     def close_all(r):
         at = pl.ds(r, STEP)
         total = parts[slot(0, 0), at] + recv_a[at].astype(F32)
-        grad_out[at] = total + recv_z[0, 0, at].astype(F32) + recv_z[1, 0, at].astype(F32)
+        grad_out[at] = (total + recv_z[0, 0, at].astype(F32) + recv_z[1, 0, at].astype(F32)) * scale
 
     loop_rows(ROWS_A, close_all)
     arrived("keys")
@@ -305,18 +381,24 @@
         hidden_remote(q).wait_send()
 
 
-def exchange(hidden, masked, weights):
-    tok, width = masked.shape
+def exchange(hidden, tokens, key_grad, weights, anchor, fragment):
+    tok, width = key_grad.shape
+    half = width // 2
     vmem = pl.BlockSpec(memory_space=pltpu.VMEM)
-    count = 80
+    smem = pl.BlockSpec(memory_space=pltpu.SMEM)
+    anywhere = pl.BlockSpec(memory_space=pl.ANY)
+    hbm = pl.BlockSpec(memory_space=pltpu.HBM)
+    count = 96
+    tile = pltpu.VMEM((8, 128), F32)
     return pl.pallas_call(
         kernel,
         out_shape=(
             jax.ShapeDtypeStruct((BLOCK, width), F32),
             jax.ShapeDtypeStruct((tok, width), BF16),
+            jax.ShapeDtypeStruct((BLOCK, half), F32),
         ),
-        in_specs=[pl.BlockSpec(memory_space=pl.ANY), vmem, vmem],
-        out_specs=(vmem, vmem),
+        in_specs=[hbm] * 5 + [smem],
+        out_specs=(vmem, vmem, vmem),
         scratch_shapes=[
             pltpu.VMEM((16, 2 * tok, BLOCK), BF16),
             pltpu.VMEM((2 * tok, width), BF16),
@@ -330,17 +412,97 @@
             pltpu.VMEM((8, ROWS_B, width), BF16),
             pltpu.VMEM((ROWS_A, width), BF16),
             pltpu.VMEM((ROWS_A, width), BF16),
+            pltpu.VMEM((tok, width), BF16),
+            pltpu.VMEM((BLOCK, width), F32),
+            pltpu.VMEM((BLOCK, width), F32),
+            pltpu.VMEM(tokens.shape, jnp.int32),
+            pltpu.VMEM((BLOCK, half), F32),
+            pltpu.VMEM((NX - 1, BLOCK // NX, half), F32),
+            pltpu.VMEM((BLOCK // NX, half), F32),
+            pltpu.VMEM((BLOCK // NX, half), F32),
+            pltpu.VMEM((BLOCK, half), F32),
+            pltpu.VMEM((1 + NZ, 8, 128), F32),
+            tile,
+            tile,
+            tile,
             pltpu.SemaphoreType.DMA((16,)),
+            pltpu.SemaphoreType.DMA((4,)),
             pltpu.SemaphoreType.DMA((count,)),
             pltpu.SemaphoreType.DMA((count,)),
             pltpu.SemaphoreType.DMA((16,)),
             pltpu.SemaphoreType.DMA((16,)),
         ],
         compiler_params=pltpu.CompilerParams(
-            collective_id=0, has_side_effects=True, vmem_limit_bytes=56 * 2**20
+            collective_id=0, has_side_effects=True, vmem_limit_bytes=52 * 2**20
         ),
         cost_estimate=pl.CostEstimate(flops=13 * 10**9, bytes_accessed=16 * 2**20, transcendentals=0),
-    )(hidden, masked, weights)
+    )(hidden, tokens, key_grad, weights, anchor, fragment)
+
+
+def finish_kernel(
+    grad, delta, keys, first, second, weights, anchor, momentum, fragment, step_count,
+    keys_out, weights_out, first_out, second_out, anchor_out, momentum_out,
+    new_weights, new_first, new_second, new_anchor, new_momentum, sems,
+):
+    rows, width = grad.shape
+    half = width // 2
+    part = rows // FINISH_PARTS
+    writes = [pltpu.make_async_copy(keys, keys_out, sems.at[0])]
+    writes[0].start()
+
+    def write(src, dst, at):
+        writes.append(pltpu.make_async_copy(src.at[at], dst.at[at], sems.at[len(writes)]))
+        writes[-1].start()
+
+    steps = jnp.full((1, half), step_count[0], jnp.int32).astype(F32)
+    first_scale = 1.0 / (1.0 - jnp.exp(steps * math.log(BETA_ONE)))
+    second_scale = 1.0 / (1.0 - jnp.exp(steps * math.log(BETA_TWO)))
+    for i in range(FINISH_PARTS):
+        at = pl.ds(i * part, part)
+        gap = delta[at]
+        for h in range(FRAGS):
+            cols = pl.ds(h * half, half)
+            moved = fragment[0] == h
+            old_anchor, old_momentum = anchor[at, cols], momentum[at, cols]
+            moved_momentum = OUTER_MOMENTUM * old_momentum + gap
+            moved_anchor = old_anchor - OUTER_LR * (gap + OUTER_MOMENTUM * moved_momentum)
+            new_momentum[at, cols] = jnp.where(moved, moved_momentum, old_momentum)
+            new_anchor[at, cols] = jnp.where(moved, moved_anchor, old_anchor)
+            gradient = grad[at, cols]
+            one = BETA_ONE * first[at, cols] + (1.0 - BETA_ONE) * gradient
+            two = BETA_TWO * second[at, cols] + (1.0 - BETA_TWO) * gradient * gradient
+            new_first[at, cols] = one
+            new_second[at, cols] = two
+            ratio = one * first_scale / (jnp.sqrt(two * second_scale) + EPSILON)
+            old = weights[at, cols]
+            stepped = old - INNER_LR * (ratio + WEIGHT_DECAY * old)
+            mixed = MIX_LOCAL * stepped + (1.0 - MIX_LOCAL) * moved_anchor
+            new_weights[at, cols] = jnp.where(moved, mixed, stepped)
+        write(new_momentum, momentum_out, at)
+        write(new_anchor, anchor_out, at)
+        write(new_first, first_out, at)
+        write(new_second, second_out, at)
+        write(new_weights, weights_out, at)
+    for copy in writes:
+        copy.wait()
+
+
+FINISH_PARTS = 4
+
+
+def finish(grad, delta, keys, first, second, weights, anchor, momentum, fragment, step_count):
+    vmem = pl.BlockSpec(memory_space=pltpu.VMEM)
+    smem = pl.BlockSpec(memory_space=pltpu.SMEM)
+    anywhere = pl.BlockSpec(memory_space=pl.ANY)
+    block = jax.ShapeDtypeStruct(grad.shape, F32)
+    return pl.pallas_call(
+        finish_kernel,
+        out_shape=(jax.ShapeDtypeStruct(keys.shape, keys.dtype),) + (block,) * 5,
+        in_specs=[vmem, vmem, anywhere] + [vmem] * 5 + [smem, smem],
+        out_specs=(anywhere,) * 6,
+        scratch_shapes=[pltpu.VMEM(grad.shape, F32)] * 5 + [pltpu.SemaphoreType.DMA((1 + 5 * FINISH_PARTS,))],
+        compiler_params=pltpu.CompilerParams(vmem_limit_bytes=16 * 2**20),
+    )(grad, delta, keys, first, second, weights, anchor, momentum, fragment, step_count)
 
 
 def on_device(
@@ -355,45 +517,11 @@
     fragment,
     step_count,
 ):
-    inverse_root = 1.0 / math.sqrt(D)
-    own_weights = weights[0]
-    key_width = own_weights.shape[1]
-    frag_width = key_width // FRAGS
-    first_col = fragment[0] * frag_width
-    live_mask = token_ids[0] != 0
-    local_count = jnp.sum(live_mask.astype(F32))
-    group_count = lax.psum(local_count, "fsdp")
-    own_delta = lax.dynamic_slice_in_dim(anchor - own_weights, first_col, frag_width, 1)
-    delta = lax.psum(own_delta, "rep") / lax.axis_size("rep")
-    masked = key_grad[0] * live_mask[:, None].astype(BF16)
-    grad_sum, new_keys = exchange(hidden[0], masked, own_weights)
-    gradient = grad_sum * inverse_root / group_count
-    step_float = step_count[0].astype(F32)
-    new_first = BETA_ONE * first_moment[0] + (1.0 - BETA_ONE) * gradient
-    new_second = BETA_TWO * second_moment[0] + (1.0 - BETA_TWO) * gradient * gradient
-    ratio_term = (
-        new_first
-        / (1.0 - BETA_ONE**step_float)
-        / (jnp.sqrt(new_second / (1.0 - BETA_TWO**step_float)) + EPSILON)
+    grad, keys, delta = exchange(hidden[0], token_ids, key_grad[0], weights[0], anchor, fragment)
+    keys, new_weights, new_first, new_second, new_anchor, new_momentum = finish(
+        grad, delta, keys, first_moment[0], second_moment[0], weights[0], anchor, momentum, fragment, step_count
     )
-    stepped = own_weights - INNER_LR * (ratio_term + WEIGHT_DECAY * own_weights)
-    momentum_cols = lax.dynamic_slice_in_dim(momentum, first_col, frag_width, 1)
-    anchor_cols = lax.dynamic_slice_in_dim(anchor, first_col, frag_width, 1)
-    moved_momentum = OUTER_MOMENTUM * momentum_cols + delta
-    moved_anchor = anchor_cols - OUTER_LR * (delta + OUTER_MOMENTUM * moved_momentum)
-    stepped_cols = lax.dynamic_slice_in_dim(stepped, first_col, frag_width, 1)
-    mixed_cols = MIX_LOCAL * stepped_cols + (1.0 - MIX_LOCAL) * moved_anchor
-    new_weights = lax.dynamic_update_slice_in_dim(stepped, mixed_cols, first_col, 1)
-    new_anchor = lax.dynamic_update_slice_in_dim(anchor, moved_anchor, first_col, 1)
-    new_momentum = lax.dynamic_update_slice_in_dim(momentum, moved_momentum, first_col, 1)
-    return (
-        new_keys[None],
-        new_weights[None],
-        new_first[None],
-        new_second[None],
-        new_anchor,
-        new_momentum,
-    )
+    return keys[None], new_weights[None], new_first[None], new_second[None], new_anchor, new_momentum
 
 
 def solution(mesh):

time: 171 us -> 81.7 us (0.48)
  blocking collectives: 69.8 us -> 0 us
  between operations: 15.5 us -> 2 us
  other arithmetic: 11 us -> 0 us
  Pallas kernels: 70.3 us -> 77.9 us
    psum x1 -> x0, blocking collectives: 69.8 us -> none  [on_device(): group_count = lax.psum(local_count, 'fsdp')]
    pallas_call x1, Pallas kernels: 70.3 us -> 76.1 us  [exchange(): pl.pallas_call(kernel, out_shape=(jax.ShapeDtypeStruct((BLOCK, width), F3...]
    broadcast_in_dim x1 -> x0, other arithmetic: 3.12 us -> none  [on_device(): new_second[None]]
    dynamic_update_slice x2 -> x0, other arithmetic: 2.33 us -> none  [the longest x1 1.26 us: on_device(): lax.dynamic_update_slice_in_dim(momentum, moved_momentum, first_col, 1)]
    mul x1 -> x0, other arithmetic: 1.86 us -> none  [on_device(): masked = key_grad[0] * live_mask[:, None].astype(BF16)]
    pallas_call x0 -> x1, Pallas kernels: none -> 1.79 us  [finish(): pl.pallas_call(finish_kernel, out_shape=(jax.ShapeDtypeStruct(keys.shape,...]
  transfers between devices with their start and end apart: 1 -> 0, of which waited for: 0 -> 0; matrix products, arithmetic and copies ran while one was open for 4% -> 0% of each run, Pallas kernels for 41% -> 0%
where the time goes in v2:
time: 81.7 us; the launch traced here: 81.6 us
  Pallas kernels  77.9 us (95%)
  between operations  2 us (2%)
  local copies, waits for them, and re-layouts  1.69 us (2%)
    pallas_call x1, Pallas kernels, exchange(): pl.pallas_call(kernel, out_shape=(jax.ShapeDtypeStruct((BLOCK, width), F3...  76.1 us
    pallas_call x1, Pallas kernels, finish(): pl.pallas_call(finish_kernel, out_shape=(jax.ShapeDtypeStruct(keys.shape,...  1.79 us
    unnamed x14, local copies, waits for them, and re-layouts  1.69 us

profile of v2, /device:TPU:1, one launch (start us, length us, event | category | flops | bytes accessed | tf_op | source)
XLA Modules:
  0.0 81.6 jit_solution(1551969331885461437)
XLA Ops:
  1.9 0.0 copy-start.5
  1.9 1.0 %copy-done.5 = bf16[1,384,512]{2,1,0:T(8,128)(2,1)S(1)} copy-done((bf16[1,384,512]{2,1,0:T(8,128)(2,1)S(1)}, bf16[1,384,512]{2,1,0:T(8,128)(2,1)}, u32[]{:S(2)}) %copy-start.5) | copy-done | bytes 393240
  2.9 0.0 copy-start.6
  2.9 0.7 copy-done.6
  3.6 0.0 copy-start
  3.6 0.0 copy-start.1
  3.6 0.0 copy-start.2
  3.6 0.0 copy-start.3
  3.6 0.0 copy-start.4
  3.6 76.1 %shard_map.145 = (f32[256,512]{1,0:T(8,128)S(1)}, bf16[384,512]{1,0:T(8,128)(2,1)S(1)}, f32[256,256]{1,0:T(8,128)S(1)}) custom-call(bf16[384,8192]{1,0:T(8,128)(2,1)} %bitcast.14, s32[1,384]{1,0:T(1,128)S(1)} %copy-done.6, bf16[384,512]{1,0:T(8,128)(2,1)S(1)} %bitcast.13, f32[256,512]{1,0:T(8,128)} %bitcast.9, f32[256,512]{1,0:T(8,128)} %anchor.3, ...), custom_call_target="tpu_custom_call" | custom-call | flops 12999999488 | bytes 16777216 | tf_op jit(solution)/shard_map/pallas_call | solution.py:393
  79.7 0.0 copy-done
  79.7 0.0 copy-done.1
  79.7 0.0 copy-done.2
  79.8 0.0 copy-done.3
  79.8 0.0 copy-done.4
  79.8 1.8 %shard_map.146 = (bf16[384,512]{1,0:T(8,128)(2,1)}, f32[256,512]{1,0:T(8,128)}, f32[256,512]{1,0:T(8,128)}, f32[256,512]{1,0:T(8,128)}, f32[256,512]{1,0:T(8,128)}, /*index=5*/f32[256,512]{1,0:T(8,128)}) custom-call(f32[256,512]{1,0:T(8,128)S(1)} %get-tuple-element.15.grad, f32[256,256]{1,0:T(8,128)S(1)} %get-tuple-element.16.delta, ...), custom_call_target="tpu_custom_call" | custom-call | tf_op jit(solution)/shard_map/pallas_call | solution.py:498
Async XLA Ops:
  1.9 1.0 %copy-start.5 = (bf16[1,384,512]{2,1,0:T(8,128)(2,1)S(1)}, bf16[1,384,512]{2,1,0:T(8,128)(2,1)}, u32[]{:S(2)}) copy-start(bf16[1,384,512]{2,1,0:T(8,128)(2,1)} %param.12) | copy-start | bytes 1179652
  2.9 0.7 copy-start.6
  3.6 76.1 %copy-start = (f32[1,256,512]{2,1,0:T(8,128)S(1)}, f32[1,256,512]{2,1,0:T(8,128)}, u32[]{:S(2)}) copy-start(f32[1,256,512]{2,1,0:T(8,128)} %param.13) | copy-start | bytes 1572868
  3.6 76.1 %copy-start.1 = (f32[256,512]{1,0:T(8,128)S(1)}, f32[256,512]{1,0:T(8,128)}, u32[]{:S(2)}) copy-start(f32[256,512]{1,0:T(8,128)} %anchor.3) | copy-start | bytes 1572868
  3.6 76.1 %copy-start.2 = (f32[1,256,512]{2,1,0:T(8,128)S(1)}, f32[1,256,512]{2,1,0:T(8,128)}, u32[]{:S(2)}) copy-start(f32[1,256,512]{2,1,0:T(8,128)} %param.14) | copy-start | bytes 1572868
  3.6 76.1 %copy-start.3 = (f32[1,256,512]{2,1,0:T(8,128)S(1)}, f32[1,256,512]{2,1,0:T(8,128)}, u32[]{:S(2)}) copy-start(f32[1,256,512]{2,1,0:T(8,128)} %param.15) | copy-start | bytes 1572868
  3.6 76.1 %copy-start.4 = (f32[256,512]{1,0:T(8,128)S(1)}, f32[256,512]{1,0:T(8,128)}, u32[]{:S(2)}) copy-start(f32[256,512]{1,0:T(8,128)} %momentum.1) | copy-start | bytes 1572868

commit v3 on v2

--- a/solution.py
+++ b/solution.py
@@ -45,7 +45,7 @@
 def kernel(
     hidden, tokens, key_grad, weights, anchor, fragment, grad_out, keys_out, delta_out,
     held, grads_in, parts, wire, acc, other, send_z, recv_z, send_y, recv_y, send_a, recv_a,
-    raw_grad, raw_weights, raw_anchor, raw_tokens, differ, from_x, piece, from_y, delta, counts, count_mate, count_pair, count_across,
+    raw_grad, raw_weights, raw_anchor, raw_tokens, differ, from_x, piece, from_y, delta, counts, count_mate, count_pair, count_across, count_total,
     local_sem, raw_sem, send_sem, recv_sem, hid_send, hid_recv,
 ):
     tok, width = key_grad.shape
@@ -129,15 +129,16 @@
         wire[own, pl.ds(r, STEP)] = raw_weights[pl.ds(r, STEP)].astype(BF16)
 
     loop_rows(BLOCK, cast)
-    loads[1].wait()
-    in_second = fragment[0].astype(F32)
-
-    def subtract(r):
-        at = pl.ds(r, STEP)
-        gap = raw_anchor[at] - raw_weights[at]
-        differ[at] = gap[:, :half] * (1.0 - in_second) + gap[:, half:] * in_second
-
-    loop_rows(BLOCK, subtract)
+    pl.semaphore_wait(barrier, len(partners))
+
+    send("ay0", wire.at[own, rows_a], wire.at[slot(0, 1), rows_a], across)
+    for s in (1, -1):
+        send(("az", s, 1, 0), wire.at[own], wire.at[slot(-s, 0)], toward[s])
+
+    @pl.loop(0, 2)
+    def _(q):
+        hidden_remote(q).start()
+
     loads[2].wait()
     loads[3].wait()
     live = (raw_tokens[...] != 0).astype(F32)
@@ -146,18 +147,22 @@
         at = pl.ds(j * 128, 128)
         grads_in[pl.ds(0, tok), at] = raw_grad[:, at] * live_rows
     count_pair[...] = jnp.broadcast_to(jnp.sum(live, axis=1, keepdims=True), count_pair.shape)
-    pl.semaphore_wait(barrier, len(partners))
-
-    send("ay0", wire.at[own, rows_a], wire.at[slot(0, 1), rows_a], across)
-    for s in (1, -1):
-        send(("az", s, 1, 0), wire.at[own], wire.at[slot(-s, 0)], toward[s])
-    send("ayB0", wire.at[own, rows_b], wire.at[slot(0, 1), rows_b], across)
     send("count_mate", count_pair, count_mate, mate)
     send("mask", grads_in.at[pl.ds(0, tok)], grads_in.at[pl.ds(tok, tok)], mate)
 
-    @pl.loop(0, 16)
+    @pl.loop(2, 16)
     def _(q):
         hidden_remote(q).start()
+
+    loads[1].wait()
+    in_second = fragment[0].astype(F32)
+
+    def subtract(r):
+        at = pl.ds(r, STEP)
+        gap = raw_anchor[at] - raw_weights[at]
+        differ[at] = gap[:, :half] * (1.0 - in_second) + gap[:, half:] * in_second
+
+    loop_rows(BLOCK, subtract)
 
     for e in range(1, NX):
         at = pl.ds(pl.multiple_of(lax.rem(x + e, NX) * quarter, quarter), quarter)
@@ -176,22 +181,23 @@
         for e in range(1, NX):
             send(("dg", e), delta.at[own_quarter], delta.at[own_quarter], along[e])
 
-    def count_chip():
-        arrived("count_mate")
-        counts[0] = count_pair[...] + count_mate[...]
-        send("count_across", counts.at[0], count_across, across)
+    def count_hop(k):
+        if k == 1:
+            arrived("count_mate")
+            counts[0] = count_pair[...] + count_mate[...]
+        for s in (1, -1):
+            if k > 1:
+                arrived(("cz", s, k - 1))
+            if k < 4 or s == 1:
+                send(("cz", s, k), counts.at[(-s * (k - 1)) % NZ], counts.at[(-s * k) % NZ], toward[s])
 
     def count_column():
-        arrived("count_across")
-        counts[1] = counts[0] + count_across[...]
-        for s in (1, -1):
-            send(("cz", s, 1), counts.at[1], counts.at[1 + (-s) % NZ], toward[s])
-
-    def count_hop(k):
-        for s in (1, -1):
-            arrived(("cz", s, k - 1))
-            if k < 4 or s == 1:
-                send(("cz", s, k), counts.at[1 + (-s * (k - 1)) % NZ], counts.at[1 + (-s * k) % NZ], toward[s])
+        arrived(("cz", 1, 4))
+        total = counts[0]
+        for i in range(1, NZ):
+            total = total + counts[i]
+        count_total[...] = total
+        send("count_across", count_total, count_across, across)
 
     def gather_hop(k, p):
         for s in (1, -1):
@@ -208,6 +214,7 @@
                 send(("ayB", src), wire.at[src, rows_b], wire.at[src + 1, rows_b], across)
 
     def gather_step(k):
+        count_hop(k)
         gather_hop(k, 0)
         gather_hop(k, 1)
 
@@ -229,7 +236,10 @@
                 send_y[o, pl.ds(r, STEP)] = parts[2 * o + 1, pl.ds(ROWS_A + r, STEP)].astype(BF16)
 
             loop_rows(ROWS_B, stage)
-            send(("ry", d), send_y.at[o], recv_y.at[o], across)
+
+    def part_y(*distances):
+        for d in distances:
+            send(("ry", d), send_y.at[order(d)], recv_y.at[order(d)], across)
 
     def reduce_far(p):
         for s in (1, -1):
@@ -295,41 +305,41 @@
 
     arrived("mask")
     gradient(4)
+    part_y(4)
     reduce_far(1)
+    count_hop(1)
     arrived("ay0")
     gather_hop(1, 1)
-    count_chip()
+    send("ayB0", wire.at[own, rows_b], wire.at[slot(0, 1), rows_b], across)
     gradient(3, -3)
+    part_y(3, -3)
+    count_hop(2)
+    gather_hop(2, 0)
     reduce_far(0)
-    gather_step(2)
+    gather_hop(2, 1)
     difference_x()
-    count_column()
     gradient(2, -2)
+    part_y(2, -2)
     reduce_hop(3, 1)
     reduce_hop(3, 0)
     gather_step(3)
-    count_hop(2)
     difference_y()
     gradient(1, -1, 0)
+    part_y(1, -1)
     acc[...] = jnp.zeros_like(acc)
     reduce_hop(2, 1)
     reduce_hop(2, 0)
     gather_step(4)
-    count_hop(3)
+    part_y(0)
     keys(0)
     reduce_hop(1, 1)
     reduce_hop(1, 0)
-    count_hop(4)
+    count_column()
     for s in (1, -1):
         arrived(("az", s, 4, 0))
         src = slot(4, 0)
         send(("ayB", 4, s), wire.at[src, rows_b, cols[s]], wire.at[src + 1, rows_b, cols[s]], across)
     keys(1, -1, 2, -2, 3, -3)
-    arrived(("cz", 1, 4))
-    group_count = counts[1]
-    for i in range(1, NZ):
-        group_count = group_count + counts[1 + i]
-    scale = ((1.0 / math.sqrt(D)) / group_count)[0:1, 0:1]
     for e in range(1, NX):
         arrived(("dg", e))
     delta_out[...] = delta[...]
@@ -346,6 +356,8 @@
     send("rya", send_a, recv_a, across)
     for s in (1, -1):
         arrived(("az", s, 4, 1))
+    arrived("count_across")
+    scale = ((1.0 / math.sqrt(D)) / (count_total[...] + count_across[...]))[0:1, 0:1]
     keys(4)
     send("keys", acc.at[pl.ds(tok, tok)], other, mate)
     for s in (1, -1):
@@ -421,7 +433,8 @@
             pltpu.VMEM((BLOCK // NX, half), F32),
             pltpu.VMEM((BLOCK // NX, half), F32),
             pltpu.VMEM((BLOCK, half), F32),
-            pltpu.VMEM((1 + NZ, 8, 128), F32),
+            pltpu.VMEM((NZ, 8, 128), F32),
+            tile,
             tile,
             tile,
             tile,
@@ -433,7 +446,7 @@
             pltpu.SemaphoreType.DMA((16,)),
         ],
         compiler_params=pltpu.CompilerParams(
-            collective_id=0, has_side_effects=True, vmem_limit_bytes=52 * 2**20
+            collective_id=0, has_side_effects=True, vmem_limit_bytes=46 * 2**20
         ),
         cost_estimate=pl.CostEstimate(flops=13 * 10**9, bytes_accessed=16 * 2**20, transcendentals=0),
     )(hidden, tokens, key_grad, weights, anchor, fragment)
@@ -517,7 +530,11 @@
     fragment,
     step_count,
 ):
-    grad, keys, delta = exchange(hidden[0], token_ids, key_grad[0], weights[0], anchor, fragment)
+    operands = [
+        pltpu.with_memory_space_constraint(operand, pltpu.HBM)
+        for operand in (hidden[0], token_ids, key_grad[0], weights[0], anchor)
+    ]
+    grad, keys, delta = exchange(*operands, fragment)
     keys, new_weights, new_first, new_second, new_anchor, new_momentum = finish(
         grad, delta, keys, first_moment[0], second_moment[0], weights[0], anchor, momentum, fragment, step_count
     )

time: 81.7 us -> 77.1 us (0.944)
  Pallas kernels: 77.9 us -> 75 us
  local copies, waits for them, and re-layouts: 1.69 us -> 0.02 us
    pallas_call x1, Pallas kernels: 76.1 us -> 73.2 us  [exchange(): pl.pallas_call(kernel, out_shape=(jax.ShapeDtypeStruct((BLOCK, width), F3...]
    unnamed x14 -> x10, local copies, waits for them, and re-layouts: 1.69 us -> 0.02 us
where the time goes in v3:
time: 77.1 us; the launch traced here: 77 us
  Pallas kernels  75 us (97%)
  between operations  2.01 us (3%)
    pallas_call x1, Pallas kernels, exchange(): pl.pallas_call(kernel, out_shape=(jax.ShapeDtypeStruct((BLOCK, width), F3...  73.2 us
    pallas_call x1, Pallas kernels, finish(): pl.pallas_call(finish_kernel, out_shape=(jax.ShapeDtypeStruct(keys.shape,...  1.79 us

profile of v3, /device:TPU:1, one launch (start us, length us, event | category | flops | bytes accessed | tf_op | source)
XLA Modules:
  0.0 77.0 jit_solution(15881478605026857137)
XLA Ops:
  1.9 0.0 copy-start
  1.9 0.0 copy-start.1
  1.9 0.0 copy-start.2
  2.0 0.0 copy-start.3
  2.0 0.0 copy-start.4
  2.0 73.2 %shard_map.145 = (f32[256,512]{1,0:T(8,128)S(1)}, bf16[384,512]{1,0:T(8,128)(2,1)S(1)}, f32[256,256]{1,0:T(8,128)S(1)}) custom-call(bf16[384,8192]{1,0:T(8,128)(2,1)} %bitcast.13, s32[1,384]{1,0:T(1,128)} %tokens.1, bf16[384,512]{1,0:T(8,128)(2,1)} %bitcast.17, f32[256,512]{1,0:T(8,128)} %bitcast.9, f32[256,512]{1,0:T(8,128)} %anchor.3, s32[1]{0:T(128)S(6)} %copy.16.fragment), custom_call_target="tpu_custom_call" | custom-call | flops 12999999488 | bytes 16777216 | tf_op jit(solution)/shard_map/pallas_call | solution.py:405
  75.2 0.0 copy-done
  75.2 0.0 copy-done.1
  75.2 0.0 copy-done.2
  75.2 0.0 copy-done.3
  75.2 0.0 copy-done.4
  75.2 1.8 %shard_map.146 = (bf16[384,512]{1,0:T(8,128)(2,1)}, f32[256,512]{1,0:T(8,128)}, f32[256,512]{1,0:T(8,128)}, f32[256,512]{1,0:T(8,128)}, f32[256,512]{1,0:T(8,128)}, /*index=5*/f32[256,512]{1,0:T(8,128)}) custom-call(f32[256,512]{1,0:T(8,128)S(1)} %get-tuple-element.15.grad, f32[256,256]{1,0:T(8,128)S(1)} %get-tuple-element.16.delta, ...), custom_call_target="tpu_custom_call" | custom-call | tf_op jit(solution)/shard_map/pallas_call | solution.py:511
Async XLA Ops:
  1.9 73.3 %copy-start = (f32[1,256,512]{2,1,0:T(8,128)S(1)}, f32[1,256,512]{2,1,0:T(8,128)}, u32[]{:S(2)}) copy-start(f32[1,256,512]{2,1,0:T(8,128)} %param.13) | copy-start | bytes 1572868
  1.9 73.3 %copy-start.1 = (f32[256,512]{1,0:T(8,128)S(1)}, f32[256,512]{1,0:T(8,128)}, u32[]{:S(2)}) copy-start(f32[256,512]{1,0:T(8,128)} %anchor.3) | copy-start | bytes 1572868
  1.9 73.3 %copy-start.2 = (f32[1,256,512]{2,1,0:T(8,128)S(1)}, f32[1,256,512]{2,1,0:T(8,128)}, u32[]{:S(2)}) copy-start(f32[1,256,512]{2,1,0:T(8,128)} %param.14) | copy-start | bytes 1572868
  2.0 73.3 %copy-start.3 = (f32[1,256,512]{2,1,0:T(8,128)S(1)}, f32[1,256,512]{2,1,0:T(8,128)}, u32[]{:S(2)}) copy-start(f32[1,256,512]{2,1,0:T(8,128)} %param.15) | copy-start | bytes 1572868
  2.0 73.3 %copy-start.4 = (f32[256,512]{1,0:T(8,128)S(1)}, f32[256,512]{1,0:T(8,128)}, u32[]{:S(2)}) copy-start(f32[256,512]{1,0:T(8,128)} %momentum.1) | copy-start | bytes 1572868

commit v4 on v3

--- a/solution.py
+++ b/solution.py
@@ -328,18 +328,19 @@
     part_y(1, -1)
     acc[...] = jnp.zeros_like(acc)
     reduce_hop(2, 1)
+    gather_step(4)
     reduce_hop(2, 0)
-    gather_step(4)
-    part_y(0)
     keys(0)
     reduce_hop(1, 1)
-    reduce_hop(1, 0)
     count_column()
     for s in (1, -1):
         arrived(("az", s, 4, 0))
         src = slot(4, 0)
         send(("ayB", 4, s), wire.at[src, rows_b, cols[s]], wire.at[src + 1, rows_b, cols[s]], across)
-    keys(1, -1, 2, -2, 3, -3)
+    part_y(0)
+    keys(1, -1)
+    reduce_hop(1, 0)
+    keys(2, -2, 3, -3)
     for e in range(1, NX):
         arrived(("dg", e))
     delta_out[...] = delta[...]
@@ -360,6 +361,13 @@
     scale = ((1.0 / math.sqrt(D)) / (count_total[...] + count_across[...]))[0:1, 0:1]
     keys(4)
     send("keys", acc.at[pl.ds(tok, tok)], other, mate)
+    arrived("keys")
+
+    def close_keys(r):
+        at = pl.ds(r, STEP)
+        keys_out[at] = ((acc[at] + other[at]) * (1.0 / math.sqrt(D))).astype(BF16)
+
+    loop_rows(tok, close_keys)
     for s in (1, -1):
         arrived(("rz", s, 1, 0))
     arrived(("ry", 0))
@@ -378,13 +386,6 @@
         grad_out[at] = (total + recv_z[0, 0, at].astype(F32) + recv_z[1, 0, at].astype(F32)) * scale
 
     loop_rows(ROWS_A, close_all)
-    arrived("keys")
-
-    def close_keys(r):
-        at = pl.ds(r, STEP)
-        keys_out[at] = ((acc[at] + other[at]) * (1.0 / math.sqrt(D))).astype(BF16)
-
-    loop_rows(tok, close_keys)
     for copy in copies.values():
         copy.wait_send()
 

time: 77.1 us -> 74.7 us (0.969)
  Pallas kernels: 75 us -> 72 us
    pallas_call x1, Pallas kernels: 73.2 us -> 70.3 us  [exchange(): pl.pallas_call(kernel, out_shape=(jax.ShapeDtypeStruct((BLOCK, width), F3...]
where the time goes in v4:
time: 74.7 us; the launch traced here: 74.1 us
  Pallas kernels  72 us (96%)
  between operations  2.01 us (3%)
    pallas_call x1, Pallas kernels, exchange(): pl.pallas_call(kernel, out_shape=(jax.ShapeDtypeStruct((BLOCK, width), F3...  70.3 us
    pallas_call x1, Pallas kernels, finish(): pl.pallas_call(finish_kernel, out_shape=(jax.ShapeDtypeStruct(keys.shape,...  1.79 us

profile of v4, /device:TPU:1, one launch (start us, length us, event | category | flops | bytes accessed | tf_op | source)
XLA Modules:
  0.0 74.1 jit_solution(13374294493452303307)
XLA Ops:
  1.9 0.0 copy-start
  1.9 0.0 copy-start.1
  1.9 0.0 copy-start.2
  2.0 0.0 copy-start.3
  2.0 0.0 copy-start.4
  2.0 70.3 %shard_map.145 = (f32[256,512]{1,0:T(8,128)S(1)}, bf16[384,512]{1,0:T(8,128)(2,1)S(1)}, f32[256,256]{1,0:T(8,128)S(1)}) custom-call(bf16[384,8192]{1,0:T(8,128)(2,1)} %bitcast.13, s32[1,384]{1,0:T(1,128)} %tokens.1, bf16[384,512]{1,0:T(8,128)(2,1)} %bitcast.17, f32[256,512]{1,0:T(8,128)} %bitcast.9, f32[256,512]{1,0:T(8,128)} %anchor.3, s32[1]{0:T(128)S(6)} %copy.16.fragment), custom_call_target="tpu_custom_call" | custom-call | flops 12999999488 | bytes 16777216 | tf_op jit(solution)/shard_map/pallas_call | solution.py:406
  72.2 0.0 copy-done
  72.2 0.0 copy-done.1
  72.3 0.0 copy-done.2
  72.3 0.0 copy-done.3
  72.3 0.0 copy-done.4
  72.3 1.8 %shard_map.146 = (bf16[384,512]{1,0:T(8,128)(2,1)}, f32[256,512]{1,0:T(8,128)}, f32[256,512]{1,0:T(8,128)}, f32[256,512]{1,0:T(8,128)}, f32[256,512]{1,0:T(8,128)}, /*index=5*/f32[256,512]{1,0:T(8,128)}) custom-call(f32[256,512]{1,0:T(8,128)S(1)} %get-tuple-element.15.grad, f32[256,256]{1,0:T(8,128)S(1)} %get-tuple-element.16.delta, ...), custom_call_target="tpu_custom_call" | custom-call | tf_op jit(solution)/shard_map/pallas_call | solution.py:512
Async XLA Ops:
  1.9 70.3 %copy-start = (f32[1,256,512]{2,1,0:T(8,128)S(1)}, f32[1,256,512]{2,1,0:T(8,128)}, u32[]{:S(2)}) copy-start(f32[1,256,512]{2,1,0:T(8,128)} %param.13) | copy-start | bytes 1572868
  1.9 70.3 %copy-start.1 = (f32[256,512]{1,0:T(8,128)S(1)}, f32[256,512]{1,0:T(8,128)}, u32[]{:S(2)}) copy-start(f32[256,512]{1,0:T(8,128)} %anchor.3) | copy-start | bytes 1572868
  1.9 70.3 %copy-start.2 = (f32[1,256,512]{2,1,0:T(8,128)S(1)}, f32[1,256,512]{2,1,0:T(8,128)}, u32[]{:S(2)}) copy-start(f32[1,256,512]{2,1,0:T(8,128)} %param.14) | copy-start | bytes 1572868
  2.0 70.3 %copy-start.3 = (f32[1,256,512]{2,1,0:T(8,128)S(1)}, f32[1,256,512]{2,1,0:T(8,128)}, u32[]{:S(2)}) copy-start(f32[1,256,512]{2,1,0:T(8,128)} %param.15) | copy-start | bytes 1572868
  2.0 70.3 %copy-start.4 = (f32[256,512]{1,0:T(8,128)S(1)}, f32[256,512]{1,0:T(8,128)}, u32[]{:S(2)}) copy-start(f32[256,512]{1,0:T(8,128)} %momentum.1) | copy-start | bytes 1572868

commit v5 on v4

--- a/solution.py
+++ b/solution.py
@@ -15,7 +15,8 @@
 NZ = 8
 NX = 4
 BLOCK = 256
-ROWS_A = 112
+ROWS_G = 144
+ROWS_A = 80
 ROWS_B = BLOCK - ROWS_A
 STEP = 16
 
@@ -62,7 +63,7 @@
     toward = {1: up, -1: down}
     beside = ((1 - yl) * NX + x, me)
     along = {e: (yl * NX + lax.rem(x + e, NX), me) for e in range(1, NX)}
-    rows_a, rows_b = pl.ds(0, ROWS_A), pl.ds(ROWS_A, ROWS_B)
+    rows_a, rows_b = pl.ds(0, ROWS_G), pl.ds(ROWS_G, BLOCK - ROWS_G)
     cols = {1: pl.ds(0, half), -1: pl.ds(half, half)}
     copies = {}
 
@@ -107,6 +108,10 @@
         def _(i):
             body(pl.multiple_of(i * STEP, STEP))
 
+    barrier = pltpu.get_barrier_semaphore()
+    partners = (mate, across, up, down, beside, *along.values())
+    for target in partners:
+        pl.semaphore_signal(barrier, inc=1, device_id=target, device_id_type=MESH)
     loads = [
         pltpu.make_async_copy(src, dst, raw_sem.at[i])
         for i, (src, dst) in enumerate(((weights, raw_weights), (anchor, raw_anchor), (key_grad, raw_grad), (tokens, raw_tokens)))
@@ -114,26 +119,22 @@
     for load in loads:
         load.start()
 
+    own = slot(0, 0)
+    loads[0].wait()
+
+    def cast(r):
+        wire[own, pl.ds(r, STEP)] = raw_weights[pl.ds(r, STEP)].astype(BF16)
+
+    loop_rows(BLOCK, cast)
+    pl.semaphore_wait(barrier, len(partners))
+
+    send("ay0", wire.at[own, rows_a], wire.at[slot(0, 1), rows_a], across)
+    for s in (1, -1):
+        send(("az", s, 1, 0), wire.at[own], wire.at[slot(-s, 0)], toward[s])
+
     @pl.loop(0, 16)
     def _(q):
         hidden_local(q).start()
-
-    barrier = pltpu.get_barrier_semaphore()
-    partners = (mate, across, up, down, beside, *along.values())
-    for target in partners:
-        pl.semaphore_signal(barrier, inc=1, device_id=target, device_id_type=MESH)
-    own = slot(0, 0)
-    loads[0].wait()
-
-    def cast(r):
-        wire[own, pl.ds(r, STEP)] = raw_weights[pl.ds(r, STEP)].astype(BF16)
-
-    loop_rows(BLOCK, cast)
-    pl.semaphore_wait(barrier, len(partners))
-
-    send("ay0", wire.at[own, rows_a], wire.at[slot(0, 1), rows_a], across)
-    for s in (1, -1):
-        send(("az", s, 1, 0), wire.at[own], wire.at[slot(-s, 0)], toward[s])
 
     @pl.loop(0, 2)
     def _(q):

time: 74.7 us -> 73.7 us (0.987)
    pallas_call x1, Pallas kernels: 70.3 us -> 69.5 us  [exchange(): pl.pallas_call(kernel, out_shape=(jax.ShapeDtypeStruct((BLOCK, width), F3...]
where the time goes in v5:
time: 73.7 us; the launch traced here: 73.3 us
  Pallas kernels  71.3 us (97%)
  between operations  2.01 us (3%)
    pallas_call x1, Pallas kernels, exchange(): pl.pallas_call(kernel, out_shape=(jax.ShapeDtypeStruct((BLOCK, width), F3...  69.5 us
    pallas_call x1, Pallas kernels, finish(): pl.pallas_call(finish_kernel, out_shape=(jax.ShapeDtypeStruct(keys.shape,...  1.79 us

profile of v5, /device:TPU:1, one launch (start us, length us, event | category | flops | bytes accessed | tf_op | source)
XLA Modules:
  0.0 73.3 jit_solution(9064321829447265621)
XLA Ops:
  1.9 0.0 copy-start
  1.9 0.0 copy-start.1
  1.9 0.0 copy-start.2
  2.0 0.0 copy-start.3
  2.0 0.0 copy-start.4
  2.0 69.5 %shard_map.145 = (f32[256,512]{1,0:T(8,128)S(1)}, bf16[384,512]{1,0:T(8,128)(2,1)S(1)}, f32[256,256]{1,0:T(8,128)S(1)}) custom-call(bf16[384,8192]{1,0:T(8,128)(2,1)} %bitcast.13, s32[1,384]{1,0:T(1,128)} %tokens.1, bf16[384,512]{1,0:T(8,128)(2,1)} %bitcast.17, f32[256,512]{1,0:T(8,128)} %bitcast.9, f32[256,512]{1,0:T(8,128)} %anchor.3, s32[1]{0:T(128)S(6)} %copy.16.fragment), custom_call_target="tpu_custom_call" | custom-call | flops 12999999488 | bytes 16777216 | tf_op jit(solution)/shard_map/pallas_call | solution.py:407
  71.5 0.0 copy-done
  71.5 0.0 copy-done.1
  71.5 0.0 copy-done.2
  71.5 0.0 copy-done.3
  71.5 0.0 copy-done.4
  71.5 1.8 %shard_map.146 = (bf16[384,512]{1,0:T(8,128)(2,1)}, f32[256,512]{1,0:T(8,128)}, f32[256,512]{1,0:T(8,128)}, f32[256,512]{1,0:T(8,128)}, f32[256,512]{1,0:T(8,128)}, /*index=5*/f32[256,512]{1,0:T(8,128)}) custom-call(f32[256,512]{1,0:T(8,128)S(1)} %get-tuple-element.15.grad, f32[256,256]{1,0:T(8,128)S(1)} %get-tuple-element.16.delta, ...), custom_call_target="tpu_custom_call" | custom-call | tf_op jit(solution)/shard_map/pallas_call | solution.py:513
Async XLA Ops:
  1.9 69.6 %copy-start = (f32[1,256,512]{2,1,0:T(8,128)S(1)}, f32[1,256,512]{2,1,0:T(8,128)}, u32[]{:S(2)}) copy-start(f32[1,256,512]{2,1,0:T(8,128)} %param.13) | copy-start | bytes 1572868
  1.9 69.6 %copy-start.1 = (f32[256,512]{1,0:T(8,128)S(1)}, f32[256,512]{1,0:T(8,128)}, u32[]{:S(2)}) copy-start(f32[256,512]{1,0:T(8,128)} %anchor.3) | copy-start | bytes 1572868
  1.9 69.6 %copy-start.2 = (f32[1,256,512]{2,1,0:T(8,128)S(1)}, f32[1,256,512]{2,1,0:T(8,128)}, u32[]{:S(2)}) copy-start(f32[1,256,512]{2,1,0:T(8,128)} %param.14) | copy-start | bytes 1572868
  2.0 69.6 %copy-start.3 = (f32[1,256,512]{2,1,0:T(8,128)S(1)}, f32[1,256,512]{2,1,0:T(8,128)}, u32[]{:S(2)}) copy-start(f32[1,256,512]{2,1,0:T(8,128)} %param.15) | copy-start | bytes 1572868
  2.0 69.6 %copy-start.4 = (f32[256,512]{1,0:T(8,128)S(1)}, f32[256,512]{1,0:T(8,128)}, u32[]{:S(2)}) copy-start(f32[256,512]{1,0:T(8,128)} %momentum.1) | copy-start | bytes 1572868

commit v6 on v5

--- a/solution.py
+++ b/solution.py
@@ -15,8 +15,8 @@
 NZ = 8
 NX = 4
 BLOCK = 256
-ROWS_G = 144
-ROWS_A = 80
+ROWS_G = 160
+ROWS_A = 64
 ROWS_B = BLOCK - ROWS_A
 STEP = 16
 

time: 73.7 us -> 73.6 us (level)
  no operation moved by 1% of the time
where the time goes in v6:
time: 73.6 us; the launch traced here: 73.5 us
  Pallas kernels  71.4 us (97%)
  between operations  2.01 us (3%)
    pallas_call x1, Pallas kernels, exchange(): pl.pallas_call(kernel, out_shape=(jax.ShapeDtypeStruct((BLOCK, width), F3...  69.6 us
    pallas_call x1, Pallas kernels, finish(): pl.pallas_call(finish_kernel, out_shape=(jax.ShapeDtypeStruct(keys.shape,...  1.79 us

profile of v6, /device:TPU:1, one launch (start us, length us, event | category | flops | bytes accessed | tf_op | source)
XLA Modules:
  0.0 73.5 jit_solution(9678917537917148296)
XLA Ops:
  1.9 0.0 copy-start
  1.9 0.0 copy-start.1
  1.9 0.0 copy-start.2
  2.0 0.0 copy-start.3
  2.0 0.0 copy-start.4
  2.0 69.6 %shard_map.145 = (f32[256,512]{1,0:T(8,128)S(1)}, bf16[384,512]{1,0:T(8,128)(2,1)S(1)}, f32[256,256]{1,0:T(8,128)S(1)}) custom-call(bf16[384,8192]{1,0:T(8,128)(2,1)} %bitcast.13, s32[1,384]{1,0:T(1,128)} %tokens.1, bf16[384,512]{1,0:T(8,128)(2,1)} %bitcast.17, f32[256,512]{1,0:T(8,128)} %bitcast.9, f32[256,512]{1,0:T(8,128)} %anchor.3, s32[1]{0:T(128)S(6)} %copy.16.fragment), custom_call_target="tpu_custom_call" | custom-call | flops 12999999488 | bytes 16777216 | tf_op jit(solution)/shard_map/pallas_call | solution.py:407
  71.6 0.0 copy-done
  71.6 0.0 copy-done.1
  71.6 0.0 copy-done.2
  71.6 0.0 copy-done.3
  71.7 0.0 copy-done.4
  71.7 1.8 %shard_map.146 = (bf16[384,512]{1,0:T(8,128)(2,1)}, f32[256,512]{1,0:T(8,128)}, f32[256,512]{1,0:T(8,128)}, f32[256,512]{1,0:T(8,128)}, f32[256,512]{1,0:T(8,128)}, /*index=5*/f32[256,512]{1,0:T(8,128)}) custom-call(f32[256,512]{1,0:T(8,128)S(1)} %get-tuple-element.15.grad, f32[256,256]{1,0:T(8,128)S(1)} %get-tuple-element.16.delta, ...), custom_call_target="tpu_custom_call" | custom-call | tf_op jit(solution)/shard_map/pallas_call | solution.py:513
Async XLA Ops:
  1.9 69.7 %copy-start = (f32[1,256,512]{2,1,0:T(8,128)S(1)}, f32[1,256,512]{2,1,0:T(8,128)}, u32[]{:S(2)}) copy-start(f32[1,256,512]{2,1,0:T(8,128)} %param.13) | copy-start | bytes 1572868
  1.9 69.7 %copy-start.1 = (f32[256,512]{1,0:T(8,128)S(1)}, f32[256,512]{1,0:T(8,128)}, u32[]{:S(2)}) copy-start(f32[256,512]{1,0:T(8,128)} %anchor.3) | copy-start | bytes 1572868
  1.9 69.7 %copy-start.2 = (f32[1,256,512]{2,1,0:T(8,128)S(1)}, f32[1,256,512]{2,1,0:T(8,128)}, u32[]{:S(2)}) copy-start(f32[1,256,512]{2,1,0:T(8,128)} %param.14) | copy-start | bytes 1572868
  2.0 69.7 %copy-start.3 = (f32[1,256,512]{2,1,0:T(8,128)S(1)}, f32[1,256,512]{2,1,0:T(8,128)}, u32[]{:S(2)}) copy-start(f32[1,256,512]{2,1,0:T(8,128)} %param.15) | copy-start | bytes 1572868
  2.0 69.7 %copy-start.4 = (f32[256,512]{1,0:T(8,128)S(1)}, f32[256,512]{1,0:T(8,128)}, u32[]{:S(2)}) copy-start(f32[256,512]{1,0:T(8,128)} %momentum.1) | copy-start | bytes 1572868
